TPU v7x, 128 devices: a whole 4x4x4 slice. The times are simulated.
128 devices in a mesh: chan: 8 (over x, core), stn: 16 (over y, z).
Axes of the slice: x: 4, y: 4, z: 4, core: 2. Of those that a mesh axis runs over, the one named last changes fastest.
Arguments:
- voltages: bfloat16 [2, 1024, 535552], P(None, ('stn', 'chan')), may hold values from -6 to 6
- fir_taps: float32 [12, 1024], replicated, may hold values from -1.75 to 1.75
- band_start: int32 [8], replicated, may hold values from 0 to 1008, as said below
- band_count: int32 [8], replicated, may hold values from 1 to 16, as said below
- subarray: int32 [512], replicated, may hold values from 0 to 3
Outputs:
- visibilities: float32 [1024, 2, 128, 1024], P('stn', None, 'chan')
Inputs may be any that keep to these rules, and one draw needn't show every extreme that they name: `band_start`: ranges of different groups may intersect; some group's range starts at channel 1024 - 16. `band_count`: one group has exactly 16 channels and another exactly 1.
All inputs are finite; a program needn't handle non-finite values.
Results may differ from a plain program's by a relative error of at most 0.0038.
Values may be sent and summed in bfloat16 or wider, within the bound.
A program may use at most 512 MiB of HBM per device.

v0:
```python
import math
import jax
import jax.numpy as jnp
from jax import lax
from jax.sharding import PartitionSpec as P

NFFT = 1024
TAPS = 12
SPECTRA = 512
CMAX = 16


def make_table(band_start, band_count):
    groups = band_start.shape[0]
    slot_ids = jnp.arange(groups * CMAX, dtype=jnp.int32)
    group_of = slot_ids // CMAX
    offset = slot_ids % CMAX
    onehot = (group_of[:, None] == jnp.arange(groups, dtype=jnp.int32)[None, :]).astype(jnp.int32)
    first_chan = jnp.sum(onehot * band_start[None, :], axis=1)
    chan_count = jnp.sum(onehot * band_count[None, :], axis=1)
    channel = first_chan + offset
    live_mask = (offset < chan_count).astype(jnp.float32)
    phase_int = jnp.arange(NFFT, dtype=jnp.int32)[None, :] * channel[:, None] % NFFT
    angles = phase_int.astype(jnp.float32) * jnp.float32(2.0 * math.pi / NFFT)
    scaling = live_mask[:, None] * jnp.float32(1.0 / math.sqrt(NFFT))
    cosine = jnp.cos(angles) * scaling
    sine_part = jnp.sin(angles) * scaling
    stacked = jnp.stack(
        [jnp.stack([cosine, sine_part], axis=1), jnp.stack([-sine_part, cosine], axis=1)], axis=1
    )
    return stacked.astype(jnp.bfloat16)


def filter_frames(volt_block, fir_taps):
    width = volt_block.shape[1]
    framed = volt_block.reshape(2, width, SPECTRA + TAPS - 1, NFFT)

    def add_tap(tap_index, summed):
        window = lax.dynamic_slice_in_dim(framed, tap_index, SPECTRA, 2)
        weights = lax.dynamic_slice_in_dim(fir_taps, tap_index, 1, 0)
        return summed + window.astype(jnp.float32) * weights

    summed = lax.fori_loop(0, TAPS, add_tap, jnp.zeros((2, width, SPECTRA, NFFT), jnp.float32))
    return summed.astype(jnp.bfloat16)


def correlate_blocks(row_data, col_data):
    rotated = jnp.stack([row_data[:, 1], -row_data[:, 0]], axis=1)
    stacked = jnp.stack([row_data, rotated], axis=0)
    return jnp.einsum("osrit,srjt->iosj", stacked, col_data, preferred_element_type=jnp.float32)


def per_device(voltages, fir_taps, band_start, band_count, subarray):
    dft_table = make_table(band_start, band_count)
    frames = filter_frames(voltages, fir_taps)
    spectra = lax.dot_general(
        dft_table, frames, (((2, 3), (0, 3)), ((), ())), preferred_element_type=jnp.float32
    ).astype(jnp.bfloat16)
    turned = lax.all_to_all(spectra, "chan", split_axis=0, concat_axis=2, tiled=True)
    stn_index = lax.axis_index("stn")
    row_block = turned.shape[2]
    correlations = correlate_blocks(turned, lax.all_gather(turned, "stn", axis=2, tiled=True))
    stations = jnp.repeat(subarray, 2)
    own_subs = lax.dynamic_slice_in_dim(stations, stn_index * row_block, row_block, 0)
    same_array = (own_subs[:, None] == stations[None, :]).astype(jnp.float32)
    return correlations * (same_array / SPECTRA)[:, None, None, :]


def solution(mesh):
    in_specs = (P(None, ("stn", "chan"), None), P(), P(), P(), P())
    out_specs = P("stn", None, "chan", None)
    return jax.shard_map(
        per_device, mesh=mesh, in_specs=in_specs, out_specs=out_specs, check_vma=False
    )
```

profile of v0, /device:TPU:1, one launch (start us, length us, event | category | flops | bytes accessed | tf_op | source)
XLA Modules:
  0.0 787.5 jit_solution(7977719925354439112)
XLA Ops:
  6.5 0.8 select_reduce_fusion.1
  8.3 493.4 %while.14 = (s32[]{:T(128)}, f32[2,8,512,1024]{3,2,1,0:T(8,128)}, bf16[2,8,523,1024]{3,1,2,0:T(8,128)(2,1)}, f32[12,1024]{1,0:T(8,128)}, s32[]{:T(128)}, /*index=5*/s32[]{:T(128)}) while((s32[]{:T(128)}, f32[2,8,512,1024]{3,2,1,0:T(8,128)}, bf16[2,8,523,1024]{3,1,2,0:T(8,128)(2,1)}, f32[12,1024]{1,0:T(8,128)}, s32[]{:T(128)}, ...), condition=%wide.region_3.4_spmd.clone, body=%wide.region_2.3_spmd.clone.sunk | while | flops 33554432 | bytes 117452888 | solution.py:43
  8.3 13.8 %constant_dynamic-slice_fusion.4 = bf16[2,8,512,1024]{3,1,2,0:T(8,128)(2,1)} fusion(bf16[2,8,523,1024]{3,1,2,0:T(8,128)(2,1)} %get-tuple-element.170, s32[]{:T(128)} %get-tuple-element.162), kind=kLoop, calls=%fused_computation.2.clone.1 | loop fusion | bytes 33554436 | tf_op jit(solution)/shard_map/while/body/eval_jaxpr/dynamic_slice | solution.py:39
  22.2 0.8 constant_dynamic-slice_fusion.5
  22.9 19.2 %select_add_fusion.2 = f32[2,8,512,1024]{3,2,1,0:T(8,128)} fusion(f32[2,8,512,1024]{3,2,1,0:T(8,128)} %get-tuple-element.163, bf16[2,8,512,1024]{3,1,2,0:T(8,128)(2,1)} %constant_dynamic-slice_fusion.4, f32[1024]{0:T(1024)S(1)} %bitcast.49, pred[]{:T(512)S(6)} %compare.21), kind=kLoop, calls=%fused_computation.clone.1 | loop fusion | flops 33554432 | bytes 83890176 | tf_op jit(solution)/shard_map/while/body/eval_jaxpr/add | solution.py:41
  42.1 13.8 %constant_dynamic-slice_fusion.4 = bf16[2,8,512,1024]{3,1,2,0:T(8,128)(2,1)} fusion(bf16[2,8,523,1024]{3,1,2,0:T(8,128)(2,1)} %get-tuple-element.170, s32[]{:T(128)} %get-tuple-element.162), kind=kLoop, calls=%fused_computation.2.clone.1 | loop fusion | bytes 33554436 | tf_op jit(solution)/shard_map/while/body/eval_jaxpr/dynamic_slice | solution.py:39
  56.0 0.8 constant_dynamic-slice_fusion.5
  56.7 27.2 %select_add_fusion.2 = f32[2,8,512,1024]{3,2,1,0:T(8,128)} fusion(f32[2,8,512,1024]{3,2,1,0:T(8,128)} %get-tuple-element.163, bf16[2,8,512,1024]{3,1,2,0:T(8,128)(2,1)} %constant_dynamic-slice_fusion.4, f32[1024]{0:T(1024)S(1)} %bitcast.49, pred[]{:T(512)S(6)} %compare.21), kind=kLoop, calls=%fused_computation.clone.1 | loop fusion | flops 33554432 | bytes 83890176 | tf_op jit(solution)/shard_map/while/body/eval_jaxpr/add | solution.py:41
  83.9 13.8 %constant_dynamic-slice_fusion.4 = bf16[2,8,512,1024]{3,1,2,0:T(8,128)(2,1)} fusion(bf16[2,8,523,1024]{3,1,2,0:T(8,128)(2,1)} %get-tuple-element.170, s32[]{:T(128)} %get-tuple-element.162), kind=kLoop, calls=%fused_computation.2.clone.1 | loop fusion | bytes 33554436 | tf_op jit(solution)/shard_map/while/body/eval_jaxpr/dynamic_slice | solution.py:39
  97.7 0.8 constant_dynamic-slice_fusion.5
  98.5 27.2 %select_add_fusion.2 = f32[2,8,512,1024]{3,2,1,0:T(8,128)} fusion(f32[2,8,512,1024]{3,2,1,0:T(8,128)} %get-tuple-element.163, bf16[2,8,512,1024]{3,1,2,0:T(8,128)(2,1)} %constant_dynamic-slice_fusion.4, f32[1024]{0:T(1024)S(1)} %bitcast.49, pred[]{:T(512)S(6)} %compare.21), kind=kLoop, calls=%fused_computation.clone.1 | loop fusion | flops 33554432 | bytes 83890176 | tf_op jit(solution)/shard_map/while/body/eval_jaxpr/add | solution.py:41
  125.7 13.8 %constant_dynamic-slice_fusion.4 = bf16[2,8,512,1024]{3,1,2,0:T(8,128)(2,1)} fusion(bf16[2,8,523,1024]{3,1,2,0:T(8,128)(2,1)} %get-tuple-element.170, s32[]{:T(128)} %get-tuple-element.162), kind=kLoop, calls=%fused_computation.2.clone.1 | loop fusion | bytes 33554436 | tf_op jit(solution)/shard_map/while/body/eval_jaxpr/dynamic_slice | solution.py:39
  139.5 0.8 constant_dynamic-slice_fusion.5
  140.3 27.2 %select_add_fusion.2 = f32[2,8,512,1024]{3,2,1,0:T(8,128)} fusion(f32[2,8,512,1024]{3,2,1,0:T(8,128)} %get-tuple-element.163, bf16[2,8,512,1024]{3,1,2,0:T(8,128)(2,1)} %constant_dynamic-slice_fusion.4, f32[1024]{0:T(1024)S(1)} %bitcast.49, pred[]{:T(512)S(6)} %compare.21), kind=kLoop, calls=%fused_computation.clone.1 | loop fusion | flops 33554432 | bytes 83890176 | tf_op jit(solution)/shard_map/while/body/eval_jaxpr/add | solution.py:41
  167.5 13.8 %constant_dynamic-slice_fusion.4 = bf16[2,8,512,1024]{3,1,2,0:T(8,128)(2,1)} fusion(bf16[2,8,523,1024]{3,1,2,0:T(8,128)(2,1)} %get-tuple-element.170, s32[]{:T(128)} %get-tuple-element.162), kind=kLoop, calls=%fused_computation.2.clone.1 | loop fusion | bytes 33554436 | tf_op jit(solution)/shard_map/while/body/eval_jaxpr/dynamic_slice | solution.py:39
  181.3 0.8 constant_dynamic-slice_fusion.5
  182.1 27.2 %select_add_fusion.2 = f32[2,8,512,1024]{3,2,1,0:T(8,128)} fusion(f32[2,8,512,1024]{3,2,1,0:T(8,128)} %get-tuple-element.163, bf16[2,8,512,1024]{3,1,2,0:T(8,128)(2,1)} %constant_dynamic-slice_fusion.4, f32[1024]{0:T(1024)S(1)} %bitcast.49, pred[]{:T(512)S(6)} %compare.21), kind=kLoop, calls=%fused_computation.clone.1 | loop fusion | flops 33554432 | bytes 83890176 | tf_op jit(solution)/shard_map/while/body/eval_jaxpr/add | solution.py:41
  209.3 13.8 %constant_dynamic-slice_fusion.4 = bf16[2,8,512,1024]{3,1,2,0:T(8,128)(2,1)} fusion(bf16[2,8,523,1024]{3,1,2,0:T(8,128)(2,1)} %get-tuple-element.170, s32[]{:T(128)} %get-tuple-element.162), kind=kLoop, calls=%fused_computation.2.clone.1 | loop fusion | bytes 33554436 | tf_op jit(solution)/shard_map/while/body/eval_jaxpr/dynamic_slice | solution.py:39
  223.1 0.8 constant_dynamic-slice_fusion.5
  223.8 27.2 %select_add_fusion.2 = f32[2,8,512,1024]{3,2,1,0:T(8,128)} fusion(f32[2,8,512,1024]{3,2,1,0:T(8,128)} %get-tuple-element.163, bf16[2,8,512,1024]{3,1,2,0:T(8,128)(2,1)} %constant_dynamic-slice_fusion.4, f32[1024]{0:T(1024)S(1)} %bitcast.49, pred[]{:T(512)S(6)} %compare.21), kind=kLoop, calls=%fused_computation.clone.1 | loop fusion | flops 33554432 | bytes 83890176 | tf_op jit(solution)/shard_map/while/body/eval_jaxpr/add | solution.py:41
  251.0 13.8 %constant_dynamic-slice_fusion.4 = bf16[2,8,512,1024]{3,1,2,0:T(8,128)(2,1)} fusion(bf16[2,8,523,1024]{3,1,2,0:T(8,128)(2,1)} %get-tuple-element.170, s32[]{:T(128)} %get-tuple-element.162), kind=kLoop, calls=%fused_computation.2.clone.1 | loop fusion | bytes 33554436 | tf_op jit(solution)/shard_map/while/body/eval_jaxpr/dynamic_slice | solution.py:39
  264.9 0.8 constant_dynamic-slice_fusion.5
  265.6 27.2 %select_add_fusion.2 = f32[2,8,512,1024]{3,2,1,0:T(8,128)} fusion(f32[2,8,512,1024]{3,2,1,0:T(8,128)} %get-tuple-element.163, bf16[2,8,512,1024]{3,1,2,0:T(8,128)(2,1)} %constant_dynamic-slice_fusion.4, f32[1024]{0:T(1024)S(1)} %bitcast.49, pred[]{:T(512)S(6)} %compare.21), kind=kLoop, calls=%fused_computation.clone.1 | loop fusion | flops 33554432 | bytes 83890176 | tf_op jit(solution)/shard_map/while/body/eval_jaxpr/add | solution.py:41
  292.8 13.8 %constant_dynamic-slice_fusion.4 = bf16[2,8,512,1024]{3,1,2,0:T(8,128)(2,1)} fusion(bf16[2,8,523,1024]{3,1,2,0:T(8,128)(2,1)} %get-tuple-element.170, s32[]{:T(128)} %get-tuple-element.162), kind=kLoop, calls=%fused_computation.2.clone.1 | loop fusion | bytes 33554436 | tf_op jit(solution)/shard_map/while/body/eval_jaxpr/dynamic_slice | solution.py:39
  306.6 0.8 constant_dynamic-slice_fusion.5
  307.4 27.2 %select_add_fusion.2 = f32[2,8,512,1024]{3,2,1,0:T(8,128)} fusion(f32[2,8,512,1024]{3,2,1,0:T(8,128)} %get-tuple-element.163, bf16[2,8,512,1024]{3,1,2,0:T(8,128)(2,1)} %constant_dynamic-slice_fusion.4, f32[1024]{0:T(1024)S(1)} %bitcast.49, pred[]{:T(512)S(6)} %compare.21), kind=kLoop, calls=%fused_computation.clone.1 | loop fusion | flops 33554432 | bytes 83890176 | tf_op jit(solution)/shard_map/while/body/eval_jaxpr/add | solution.py:41
  334.6 13.8 %constant_dynamic-slice_fusion.4 = bf16[2,8,512,1024]{3,1,2,0:T(8,128)(2,1)} fusion(bf16[2,8,523,1024]{3,1,2,0:T(8,128)(2,1)} %get-tuple-element.170, s32[]{:T(128)} %get-tuple-element.162), kind=kLoop, calls=%fused_computation.2.clone.1 | loop fusion | bytes 33554436 | tf_op jit(solution)/shard_map/while/body/eval_jaxpr/dynamic_slice | solution.py:39
  348.4 0.8 constant_dynamic-slice_fusion.5
  349.2 27.2 %select_add_fusion.2 = f32[2,8,512,1024]{3,2,1,0:T(8,128)} fusion(f32[2,8,512,1024]{3,2,1,0:T(8,128)} %get-tuple-element.163, bf16[2,8,512,1024]{3,1,2,0:T(8,128)(2,1)} %constant_dynamic-slice_fusion.4, f32[1024]{0:T(1024)S(1)} %bitcast.49, pred[]{:T(512)S(6)} %compare.21), kind=kLoop, calls=%fused_computation.clone.1 | loop fusion | flops 33554432 | bytes 83890176 | tf_op jit(solution)/shard_map/while/body/eval_jaxpr/add | solution.py:41
  376.4 13.8 %constant_dynamic-slice_fusion.4 = bf16[2,8,512,1024]{3,1,2,0:T(8,128)(2,1)} fusion(bf16[2,8,523,1024]{3,1,2,0:T(8,128)(2,1)} %get-tuple-element.170, s32[]{:T(128)} %get-tuple-element.162), kind=kLoop, calls=%fused_computation.2.clone.1 | loop fusion | bytes 33554436 | tf_op jit(solution)/shard_map/while/body/eval_jaxpr/dynamic_slice | solution.py:39
  390.2 0.8 constant_dynamic-slice_fusion.5
  390.9 27.2 %select_add_fusion.2 = f32[2,8,512,1024]{3,2,1,0:T(8,128)} fusion(f32[2,8,512,1024]{3,2,1,0:T(8,128)} %get-tuple-element.163, bf16[2,8,512,1024]{3,1,2,0:T(8,128)(2,1)} %constant_dynamic-slice_fusion.4, f32[1024]{0:T(1024)S(1)} %bitcast.49, pred[]{:T(512)S(6)} %compare.21), kind=kLoop, calls=%fused_computation.clone.1 | loop fusion | flops 33554432 | bytes 83890176 | tf_op jit(solution)/shard_map/while/body/eval_jaxpr/add | solution.py:41
  418.1 13.8 %constant_dynamic-slice_fusion.4 = bf16[2,8,512,1024]{3,1,2,0:T(8,128)(2,1)} fusion(bf16[2,8,523,1024]{3,1,2,0:T(8,128)(2,1)} %get-tuple-element.170, s32[]{:T(128)} %get-tuple-element.162), kind=kLoop, calls=%fused_computation.2.clone.1 | loop fusion | bytes 33554436 | tf_op jit(solution)/shard_map/while/body/eval_jaxpr/dynamic_slice | solution.py:39
  432.0 0.8 constant_dynamic-slice_fusion.5
  432.7 27.2 %select_add_fusion.2 = f32[2,8,512,1024]{3,2,1,0:T(8,128)} fusion(f32[2,8,512,1024]{3,2,1,0:T(8,128)} %get-tuple-element.163, bf16[2,8,512,1024]{3,1,2,0:T(8,128)(2,1)} %constant_dynamic-slice_fusion.4, f32[1024]{0:T(1024)S(1)} %bitcast.49, pred[]{:T(512)S(6)} %compare.21), kind=kLoop, calls=%fused_computation.clone.1 | loop fusion | flops 33554432 | bytes 83890176 | tf_op jit(solution)/shard_map/while/body/eval_jaxpr/add | solution.py:41
  459.9 13.8 %constant_dynamic-slice_fusion.4 = bf16[2,8,512,1024]{3,1,2,0:T(8,128)(2,1)} fusion(bf16[2,8,523,1024]{3,1,2,0:T(8,128)(2,1)} %get-tuple-element.170, s32[]{:T(128)} %get-tuple-element.162), kind=kLoop, calls=%fused_computation.2.clone.1 | loop fusion | bytes 33554436 | tf_op jit(solution)/shard_map/while/body/eval_jaxpr/dynamic_slice | solution.py:39
  473.7 0.8 constant_dynamic-slice_fusion.5
  474.5 27.2 %select_add_fusion.2 = f32[2,8,512,1024]{3,2,1,0:T(8,128)} fusion(f32[2,8,512,1024]{3,2,1,0:T(8,128)} %get-tuple-element.163, bf16[2,8,512,1024]{3,1,2,0:T(8,128)(2,1)} %constant_dynamic-slice_fusion.4, f32[1024]{0:T(1024)S(1)} %bitcast.49, pred[]{:T(512)S(6)} %compare.21), kind=kLoop, calls=%fused_computation.clone.1 | loop fusion | flops 33554432 | bytes 83890176 | tf_op jit(solution)/shard_map/while/body/eval_jaxpr/add | solution.py:41
  501.7 2.5 fusion.22
  504.3 13.0 %bitcast_convert_fusion = bf16[128,2,8,512]{3,0,2,1:T(8,128)(2,1)S(1)} fusion(bf16[128,1,2,1024]{3,0,2,1:T(8,128)(2,1)S(1)} %get-tuple-element.127, bf16[128,1,2,1024]{3,0,2,1:T(8,128)(2,1)S(1)} %get-tuple-element.126, f32[2,8,512,1024]{3,2,1,0:T(8,128)} %get-tuple-element.84), kind=kOutput, calls=%fused_computation.12 | convolution fusion | flops 4306501632 | bytes 36700160 | tf_op jit(solution)/shard_map/dot_general | solution.py:56
  517.3 1.2 copy.22
  518.4 32.1 %all_to_all.18 = bf16[128,2,8,512]{3,2,1,0:T(8,128)(2,1)S(1)} all-to-all(bf16[128,2,8,512]{3,2,1,0:T(8,128)(2,1)S(1)} %copy.22), channel_id=1, replica_groups=mesh['chan'=8,'stn'=16] {'chan'}, dimensions={0} | all-to-all | bytes 4194304 | tf_op jit(solution)/shard_map/all_to_all | solution.py:59
  550.5 1.6 copy.39
  552.6 1.8 fusion.26
  554.4 1.5 maximum_bitcast_fusion
  555.9 194.4 %all-gather.2.cloned.1.call-done = bf16[16,2,1024,512]{3,2,1,0:T(8,128)(2,1)} async-done(((bf16[16,2,64,512]{3,2,1,0:T(8,128)(2,1)}), bf16[16,2,1024,512]{3,2,1,0:T(8,128)(2,1)}) %all-gather.2.cloned.1.call-update) | async-done | bytes 33554448 | tf_op jit(solution)/shard_map/all_gather | solution.py:62
  750.3 18.7 %bitcast_multiply_fusion = f32[64,2,16,1024]{3,0,1,2:T(8,128)} fusion(f32[64,1024]{1,0:T(8,128)S(1)} %compare_select_fusion, bf16[1,16,2,64,512]{4,3,2,0,1:T(8,128)(2,1)} %maximum_bitcast_fusion, bf16[1,16,2,64,512]{4,3,2,0,1:T(8,128)(2,1)S(1)} %bitcast.47, bf16[16,2,1024,512]{3,2,1,0:T(8,128)(2,1)} %all-gather.2.cloned.1.call-done), kind=kOutput, calls=%fused_computation.8 | convolution fusion | flops 4305453056 | bytes 46399488 | tf_op jit(solution)/shard_map/osrit,srjt->iosj/dot_general | solution.py:50
  769.1 11.6 %copy.24 = f32[64,2,16,1024]{3,2,1,0:T(8,128)} copy(f32[64,2,16,1024]{3,0,1,2:T(8,128)} %bitcast_multiply_fusion) | data formatting | bytes 16777216 | tf_op jit(solution)/shard_map/mul | solution.py:66
  (19 shorter events, 1.6 us)
Async XLA Ops:
  6.5 743.8 %all-gather.2.cloned.1.call-start = ((), (), s32[]{:S(2)}) async-start(), calls=%async_computation.1 | async-start | bytes 35651584 | tf_op jit(solution)/shard_map/all_gather | solution.py:62
  8.3 493.4 %copy-start.2 = (f32[128]{0:T(128)S(1)}, f32[128]{0:T(128)}, u32[]{:S(2)}) copy-start(f32[128]{0:T(128)} %compare_select_fusion.1) | copy-start | bytes 1540
  8.3 493.4 %copy-start.3 = (s32[128]{0:T(128)S(1)}, s32[128]{0:T(128)}, u32[]{:S(2)}) copy-start(s32[128]{0:T(128)} %fusion.23) | copy-start | bytes 1540
  517.2 34.9 %copy-start.1 = (s32[512]{0:T(512)S(1)}, s32[512]{0:T(512)}, u32[]{:S(2)}) copy-start(s32[512]{0:T(512)} %param.11) | copy-start | bytes 6148
  552.1 198.2 %copy-start = (bf16[8,16,2,8,512]{4,3,0,2,1:T(8,128)(2,1)S(1)}, bf16[8,16,2,8,512]{4,3,0,2,1:T(8,128)(2,1)}, u32[]{:S(2)}) copy-start(bf16[8,16,2,8,512]{4,3,0,2,1:T(8,128)(2,1)} %copy.39) | copy-start | bytes 6291460
Sparse Core Ops, SparseCore 0:
  552.2 198.0 all-gather.1
where the time goes:
time: 790 us; the launch traced here: 788 us
  other arithmetic  326 us (41%)
  waiting for transfers between devices  194 us (25%)
  local copies, waits for them, and re-layouts  190 us (24%)
  blocking collectives  32.1 us (4%)
  matrix products  31.7 us (4%)
  between operations  13.5 us (2%)
    add x12, other arithmetic, add_tap(): return summed + window.astype(jnp.float32) * weights  318 us
    all_gather x1, waiting for transfers between devices, per_device(): lax.all_gather(turned, 'stn', axis=2, tiled=True)  194 us
    dynamic_slice x12, local copies, waits for them, and re-layouts, add_tap(): window = lax.dynamic_slice_in_dim(framed, tap_index, SPECTRA, 2)  166 us
    all_to_all x1, blocking collectives, per_device(): lax.all_to_all(spectra, 'chan', split_axis=0, concat_axis=2, tiled=True)  32.1 us
    dot_general x1, matrix products, correlate_blocks(): jnp.einsum('osrit,srjt->iosj', stacked, col_data, preferred_element_type=...  18.7 us
  transfers between devices with their start and end apart: 1, of which 1 were waited for; matrix products, arithmetic and copies ran while one was open for 0% of the time, Pallas kernels for 0%

commit v1 on v0

--- a/solution.py
+++ b/solution.py
@@ -8,6 +8,13 @@
 TAPS = 12
 SPECTRA = 512
 CMAX = 16
+
+
+def rates_unite(sheet, chip_axis):
+    p_next = lax.psum(1, chip_axis)
+    high = jnp.stack(p_next * [sheet])
+    w1 = lax.all_to_all(high, chip_axis, 0, 0)
+    return jnp.concatenate(w1, axis=2)
 
 
 def make_table(band_start, band_count):
@@ -59,7 +66,7 @@
     turned = lax.all_to_all(spectra, "chan", split_axis=0, concat_axis=2, tiled=True)
     stn_index = lax.axis_index("stn")
     row_block = turned.shape[2]
-    correlations = correlate_blocks(turned, lax.all_gather(turned, "stn", axis=2, tiled=True))
+    correlations = correlate_blocks(turned, rates_unite(turned, "stn"))
     stations = jnp.repeat(subarray, 2)
     own_subs = lax.dynamic_slice_in_dim(stations, stn_index * row_block, row_block, 0)
     same_array = (own_subs[:, None] == stations[None, :]).astype(jnp.float32)

time: 790 us -> 1240 us (1.57)
  waiting for transfers between devices: 194 us -> 615 us
  local copies, waits for them, and re-layouts: 190 us -> 223 us
  between operations: 13.5 us -> 0.1 us
    all_to_all x0 -> x1, waiting for transfers between devices: none -> 615 us  [rates_unite(): w1 = lax.all_to_all(high, chip_axis, 0, 0)]
    all_gather x1 -> x0, waiting for transfers between devices: 194 us -> none  [per_device(): lax.all_gather(turned, 'stn', axis=2, tiled=True)]
    reshape x0 -> x1, local copies, waits for them, and re-layouts: none -> 22.9 us  [rates_unite(): return jnp.concatenate(w1, axis=2)]
where the time goes in v1:
time: 1240 us; the launch traced here: 1230 us
  waiting for transfers between devices  615 us (50%)
  other arithmetic  324 us (26%)
  local copies, waits for them, and re-layouts  223 us (18%)
  blocking collectives  32.1 us (3%)
  matrix products  31.7 us (3%)
    all_to_all x1, waiting for transfers between devices, rates_unite(): w1 = lax.all_to_all(high, chip_axis, 0, 0)  615 us
    add x12, other arithmetic, add_tap(): return summed + window.astype(jnp.float32) * weights  318 us
    dynamic_slice x12, local copies, waits for them, and re-layouts, add_tap(): window = lax.dynamic_slice_in_dim(framed, tap_index, SPECTRA, 2)  166 us
    all_to_all x1, blocking collectives, per_device(): lax.all_to_all(spectra, 'chan', split_axis=0, concat_axis=2, tiled=True)  32.1 us
  transfers between devices with their start and end apart: 1, of which 1 were waited for; matrix products, arithmetic and copies ran while one was open for 0% of the time, Pallas kernels for 0%

profile of v1, /device:TPU:1, one launch (start us, length us, event | category | flops | bytes accessed | tf_op | source)
XLA Modules:
  0.0 1234.3 jit_solution(871834451656398997)
XLA Ops:
  1.8 493.5 %while.14 = (s32[]{:T(128)}, f32[2,8,512,1024]{3,2,1,0:T(8,128)}, bf16[2,8,523,1024]{3,1,2,0:T(8,128)(2,1)}, f32[12,1024]{1,0:T(8,128)}, s32[]{:T(128)}, /*index=5*/s32[]{:T(128)}) while((s32[]{:T(128)}, f32[2,8,512,1024]{3,2,1,0:T(8,128)}, bf16[2,8,523,1024]{3,1,2,0:T(8,128)(2,1)}, f32[12,1024]{1,0:T(8,128)}, s32[]{:T(128)}, ...), condition=%wide.region_3.4_spmd.clone, body=%wide.region_2.3_spmd.clone.sunk | while | flops 33554432 | bytes 117452888 | solution.py:50
  1.8 13.8 %constant_dynamic-slice_fusion.4 = bf16[2,8,512,1024]{3,1,2,0:T(8,128)(2,1)} fusion(bf16[2,8,523,1024]{3,1,2,0:T(8,128)(2,1)} %get-tuple-element.170, s32[]{:T(128)} %get-tuple-element.162), kind=kLoop, calls=%fused_computation.2.clone.1 | loop fusion | bytes 33554436 | tf_op jit(solution)/shard_map/while/body/eval_jaxpr/dynamic_slice | solution.py:46
  15.6 0.8 constant_dynamic-slice_fusion.5
  16.4 19.2 %select_add_fusion.2 = f32[2,8,512,1024]{3,2,1,0:T(8,128)} fusion(f32[2,8,512,1024]{3,2,1,0:T(8,128)} %get-tuple-element.163, bf16[2,8,512,1024]{3,1,2,0:T(8,128)(2,1)} %constant_dynamic-slice_fusion.4, f32[1024]{0:T(1024)S(1)} %bitcast.50, pred[]{:T(512)S(6)} %compare.21), kind=kLoop, calls=%fused_computation.clone.1 | loop fusion | flops 33554432 | bytes 83890176 | tf_op jit(solution)/shard_map/while/body/eval_jaxpr/add | solution.py:48
  35.6 13.8 %constant_dynamic-slice_fusion.4 = bf16[2,8,512,1024]{3,1,2,0:T(8,128)(2,1)} fusion(bf16[2,8,523,1024]{3,1,2,0:T(8,128)(2,1)} %get-tuple-element.170, s32[]{:T(128)} %get-tuple-element.162), kind=kLoop, calls=%fused_computation.2.clone.1 | loop fusion | bytes 33554436 | tf_op jit(solution)/shard_map/while/body/eval_jaxpr/dynamic_slice | solution.py:46
  49.5 0.8 constant_dynamic-slice_fusion.5
  50.2 27.2 %select_add_fusion.2 = f32[2,8,512,1024]{3,2,1,0:T(8,128)} fusion(f32[2,8,512,1024]{3,2,1,0:T(8,128)} %get-tuple-element.163, bf16[2,8,512,1024]{3,1,2,0:T(8,128)(2,1)} %constant_dynamic-slice_fusion.4, f32[1024]{0:T(1024)S(1)} %bitcast.50, pred[]{:T(512)S(6)} %compare.21), kind=kLoop, calls=%fused_computation.clone.1 | loop fusion | flops 33554432 | bytes 83890176 | tf_op jit(solution)/shard_map/while/body/eval_jaxpr/add | solution.py:48
  77.4 13.8 %constant_dynamic-slice_fusion.4 = bf16[2,8,512,1024]{3,1,2,0:T(8,128)(2,1)} fusion(bf16[2,8,523,1024]{3,1,2,0:T(8,128)(2,1)} %get-tuple-element.170, s32[]{:T(128)} %get-tuple-element.162), kind=kLoop, calls=%fused_computation.2.clone.1 | loop fusion | bytes 33554436 | tf_op jit(solution)/shard_map/while/body/eval_jaxpr/dynamic_slice | solution.py:46
  91.2 0.8 constant_dynamic-slice_fusion.5
  92.0 27.2 %select_add_fusion.2 = f32[2,8,512,1024]{3,2,1,0:T(8,128)} fusion(f32[2,8,512,1024]{3,2,1,0:T(8,128)} %get-tuple-element.163, bf16[2,8,512,1024]{3,1,2,0:T(8,128)(2,1)} %constant_dynamic-slice_fusion.4, f32[1024]{0:T(1024)S(1)} %bitcast.50, pred[]{:T(512)S(6)} %compare.21), kind=kLoop, calls=%fused_computation.clone.1 | loop fusion | flops 33554432 | bytes 83890176 | tf_op jit(solution)/shard_map/while/body/eval_jaxpr/add | solution.py:48
  119.2 13.8 %constant_dynamic-slice_fusion.4 = bf16[2,8,512,1024]{3,1,2,0:T(8,128)(2,1)} fusion(bf16[2,8,523,1024]{3,1,2,0:T(8,128)(2,1)} %get-tuple-element.170, s32[]{:T(128)} %get-tuple-element.162), kind=kLoop, calls=%fused_computation.2.clone.1 | loop fusion | bytes 33554436 | tf_op jit(solution)/shard_map/while/body/eval_jaxpr/dynamic_slice | solution.py:46
  133.0 0.8 constant_dynamic-slice_fusion.5
  133.8 27.2 %select_add_fusion.2 = f32[2,8,512,1024]{3,2,1,0:T(8,128)} fusion(f32[2,8,512,1024]{3,2,1,0:T(8,128)} %get-tuple-element.163, bf16[2,8,512,1024]{3,1,2,0:T(8,128)(2,1)} %constant_dynamic-slice_fusion.4, f32[1024]{0:T(1024)S(1)} %bitcast.50, pred[]{:T(512)S(6)} %compare.21), kind=kLoop, calls=%fused_computation.clone.1 | loop fusion | flops 33554432 | bytes 83890176 | tf_op jit(solution)/shard_map/while/body/eval_jaxpr/add | solution.py:48
  161.0 13.8 %constant_dynamic-slice_fusion.4 = bf16[2,8,512,1024]{3,1,2,0:T(8,128)(2,1)} fusion(bf16[2,8,523,1024]{3,1,2,0:T(8,128)(2,1)} %get-tuple-element.170, s32[]{:T(128)} %get-tuple-element.162), kind=kLoop, calls=%fused_computation.2.clone.1 | loop fusion | bytes 33554436 | tf_op jit(solution)/shard_map/while/body/eval_jaxpr/dynamic_slice | solution.py:46
  174.8 0.8 constant_dynamic-slice_fusion.5
  175.6 27.2 %select_add_fusion.2 = f32[2,8,512,1024]{3,2,1,0:T(8,128)} fusion(f32[2,8,512,1024]{3,2,1,0:T(8,128)} %get-tuple-element.163, bf16[2,8,512,1024]{3,1,2,0:T(8,128)(2,1)} %constant_dynamic-slice_fusion.4, f32[1024]{0:T(1024)S(1)} %bitcast.50, pred[]{:T(512)S(6)} %compare.21), kind=kLoop, calls=%fused_computation.clone.1 | loop fusion | flops 33554432 | bytes 83890176 | tf_op jit(solution)/shard_map/while/body/eval_jaxpr/add | solution.py:48
  202.8 13.8 %constant_dynamic-slice_fusion.4 = bf16[2,8,512,1024]{3,1,2,0:T(8,128)(2,1)} fusion(bf16[2,8,523,1024]{3,1,2,0:T(8,128)(2,1)} %get-tuple-element.170, s32[]{:T(128)} %get-tuple-element.162), kind=kLoop, calls=%fused_computation.2.clone.1 | loop fusion | bytes 33554436 | tf_op jit(solution)/shard_map/while/body/eval_jaxpr/dynamic_slice | solution.py:46
  216.6 0.8 constant_dynamic-slice_fusion.5
  217.4 27.2 %select_add_fusion.2 = f32[2,8,512,1024]{3,2,1,0:T(8,128)} fusion(f32[2,8,512,1024]{3,2,1,0:T(8,128)} %get-tuple-element.163, bf16[2,8,512,1024]{3,1,2,0:T(8,128)(2,1)} %constant_dynamic-slice_fusion.4, f32[1024]{0:T(1024)S(1)} %bitcast.50, pred[]{:T(512)S(6)} %compare.21), kind=kLoop, calls=%fused_computation.clone.1 | loop fusion | flops 33554432 | bytes 83890176 | tf_op jit(solution)/shard_map/while/body/eval_jaxpr/add | solution.py:48
  244.6 13.8 %constant_dynamic-slice_fusion.4 = bf16[2,8,512,1024]{3,1,2,0:T(8,128)(2,1)} fusion(bf16[2,8,523,1024]{3,1,2,0:T(8,128)(2,1)} %get-tuple-element.170, s32[]{:T(128)} %get-tuple-element.162), kind=kLoop, calls=%fused_computation.2.clone.1 | loop fusion | bytes 33554436 | tf_op jit(solution)/shard_map/while/body/eval_jaxpr/dynamic_slice | solution.py:46
  258.4 0.8 constant_dynamic-slice_fusion.5
  259.2 27.2 %select_add_fusion.2 = f32[2,8,512,1024]{3,2,1,0:T(8,128)} fusion(f32[2,8,512,1024]{3,2,1,0:T(8,128)} %get-tuple-element.163, bf16[2,8,512,1024]{3,1,2,0:T(8,128)(2,1)} %constant_dynamic-slice_fusion.4, f32[1024]{0:T(1024)S(1)} %bitcast.50, pred[]{:T(512)S(6)} %compare.21), kind=kLoop, calls=%fused_computation.clone.1 | loop fusion | flops 33554432 | bytes 83890176 | tf_op jit(solution)/shard_map/while/body/eval_jaxpr/add | solution.py:48
  286.3 13.8 %constant_dynamic-slice_fusion.4 = bf16[2,8,512,1024]{3,1,2,0:T(8,128)(2,1)} fusion(bf16[2,8,523,1024]{3,1,2,0:T(8,128)(2,1)} %get-tuple-element.170, s32[]{:T(128)} %get-tuple-element.162), kind=kLoop, calls=%fused_computation.2.clone.1 | loop fusion | bytes 33554436 | tf_op jit(solution)/shard_map/while/body/eval_jaxpr/dynamic_slice | solution.py:46
  300.2 0.8 constant_dynamic-slice_fusion.5
  300.9 27.2 %select_add_fusion.2 = f32[2,8,512,1024]{3,2,1,0:T(8,128)} fusion(f32[2,8,512,1024]{3,2,1,0:T(8,128)} %get-tuple-element.163, bf16[2,8,512,1024]{3,1,2,0:T(8,128)(2,1)} %constant_dynamic-slice_fusion.4, f32[1024]{0:T(1024)S(1)} %bitcast.50, pred[]{:T(512)S(6)} %compare.21), kind=kLoop, calls=%fused_computation.clone.1 | loop fusion | flops 33554432 | bytes 83890176 | tf_op jit(solution)/shard_map/while/body/eval_jaxpr/add | solution.py:48
  328.1 13.8 %constant_dynamic-slice_fusion.4 = bf16[2,8,512,1024]{3,1,2,0:T(8,128)(2,1)} fusion(bf16[2,8,523,1024]{3,1,2,0:T(8,128)(2,1)} %get-tuple-element.170, s32[]{:T(128)} %get-tuple-element.162), kind=kLoop, calls=%fused_computation.2.clone.1 | loop fusion | bytes 33554436 | tf_op jit(solution)/shard_map/while/body/eval_jaxpr/dynamic_slice | solution.py:46
  342.0 0.8 constant_dynamic-slice_fusion.5
  342.7 27.2 %select_add_fusion.2 = f32[2,8,512,1024]{3,2,1,0:T(8,128)} fusion(f32[2,8,512,1024]{3,2,1,0:T(8,128)} %get-tuple-element.163, bf16[2,8,512,1024]{3,1,2,0:T(8,128)(2,1)} %constant_dynamic-slice_fusion.4, f32[1024]{0:T(1024)S(1)} %bitcast.50, pred[]{:T(512)S(6)} %compare.21), kind=kLoop, calls=%fused_computation.clone.1 | loop fusion | flops 33554432 | bytes 83890176 | tf_op jit(solution)/shard_map/while/body/eval_jaxpr/add | solution.py:48
  369.9 13.8 %constant_dynamic-slice_fusion.4 = bf16[2,8,512,1024]{3,1,2,0:T(8,128)(2,1)} fusion(bf16[2,8,523,1024]{3,1,2,0:T(8,128)(2,1)} %get-tuple-element.170, s32[]{:T(128)} %get-tuple-element.162), kind=kLoop, calls=%fused_computation.2.clone.1 | loop fusion | bytes 33554436 | tf_op jit(solution)/shard_map/while/body/eval_jaxpr/dynamic_slice | solution.py:46
  383.8 0.8 constant_dynamic-slice_fusion.5
  384.5 27.2 %select_add_fusion.2 = f32[2,8,512,1024]{3,2,1,0:T(8,128)} fusion(f32[2,8,512,1024]{3,2,1,0:T(8,128)} %get-tuple-element.163, bf16[2,8,512,1024]{3,1,2,0:T(8,128)(2,1)} %constant_dynamic-slice_fusion.4, f32[1024]{0:T(1024)S(1)} %bitcast.50, pred[]{:T(512)S(6)} %compare.21), kind=kLoop, calls=%fused_computation.clone.1 | loop fusion | flops 33554432 | bytes 83890176 | tf_op jit(solution)/shard_map/while/body/eval_jaxpr/add | solution.py:48
  411.7 13.8 %constant_dynamic-slice_fusion.4 = bf16[2,8,512,1024]{3,1,2,0:T(8,128)(2,1)} fusion(bf16[2,8,523,1024]{3,1,2,0:T(8,128)(2,1)} %get-tuple-element.170, s32[]{:T(128)} %get-tuple-element.162), kind=kLoop, calls=%fused_computation.2.clone.1 | loop fusion | bytes 33554436 | tf_op jit(solution)/shard_map/while/body/eval_jaxpr/dynamic_slice | solution.py:46
  425.5 0.8 constant_dynamic-slice_fusion.5
  426.3 27.2 %select_add_fusion.2 = f32[2,8,512,1024]{3,2,1,0:T(8,128)} fusion(f32[2,8,512,1024]{3,2,1,0:T(8,128)} %get-tuple-element.163, bf16[2,8,512,1024]{3,1,2,0:T(8,128)(2,1)} %constant_dynamic-slice_fusion.4, f32[1024]{0:T(1024)S(1)} %bitcast.50, pred[]{:T(512)S(6)} %compare.21), kind=kLoop, calls=%fused_computation.clone.1 | loop fusion | flops 33554432 | bytes 83890176 | tf_op jit(solution)/shard_map/while/body/eval_jaxpr/add | solution.py:48
  453.5 13.8 %constant_dynamic-slice_fusion.4 = bf16[2,8,512,1024]{3,1,2,0:T(8,128)(2,1)} fusion(bf16[2,8,523,1024]{3,1,2,0:T(8,128)(2,1)} %get-tuple-element.170, s32[]{:T(128)} %get-tuple-element.162), kind=kLoop, calls=%fused_computation.2.clone.1 | loop fusion | bytes 33554436 | tf_op jit(solution)/shard_map/while/body/eval_jaxpr/dynamic_slice | solution.py:46
  467.3 0.8 constant_dynamic-slice_fusion.5
  468.1 27.2 %select_add_fusion.2 = f32[2,8,512,1024]{3,2,1,0:T(8,128)} fusion(f32[2,8,512,1024]{3,2,1,0:T(8,128)} %get-tuple-element.163, bf16[2,8,512,1024]{3,1,2,0:T(8,128)(2,1)} %constant_dynamic-slice_fusion.4, f32[1024]{0:T(1024)S(1)} %bitcast.50, pred[]{:T(512)S(6)} %compare.21), kind=kLoop, calls=%fused_computation.clone.1 | loop fusion | flops 33554432 | bytes 83890176 | tf_op jit(solution)/shard_map/while/body/eval_jaxpr/add | solution.py:48
  495.3 2.5 fusion.19
  497.9 13.0 %bitcast_convert_fusion = bf16[128,2,8,512]{3,0,2,1:T(8,128)(2,1)S(1)} fusion(bf16[128,1,2,1024]{3,0,2,1:T(8,128)(2,1)S(1)} %get-tuple-element.127, bf16[128,1,2,1024]{3,0,2,1:T(8,128)(2,1)S(1)} %get-tuple-element.126, f32[2,8,512,1024]{3,2,1,0:T(8,128)} %get-tuple-element.84), kind=kOutput, calls=%fused_computation.11 | convolution fusion | flops 4306501632 | bytes 36700160 | tf_op jit(solution)/shard_map/dot_general | solution.py:63
  510.8 1.2 copy.23
  512.0 32.1 %all_to_all.20 = bf16[128,2,8,512]{3,2,1,0:T(8,128)(2,1)S(1)} all-to-all(bf16[128,2,8,512]{3,2,1,0:T(8,128)(2,1)S(1)} %copy.23), channel_id=1, replica_groups=mesh['chan'=8,'stn'=16] {'chan'}, dimensions={0} | all-to-all | bytes 4194304 | tf_op jit(solution)/shard_map/all_to_all | solution.py:66
  544.4 11.1 stack.64
  555.5 8.0 all-to-all-start.1
  564.1 1.5 maximum_bitcast_fusion
  565.6 615.4 %all-to-all-done.1 = bf16[16,16,2,64,512]{4,3,2,1,0:T(8,128)(2,1)} async-done(((bf16[16,16,2,64,512]{4,3,2,1,0:T(8,128)(2,1)}), bf16[16,16,2,64,512]{4,3,2,1,0:T(8,128)(2,1)}, u32[]{:S(2)}, u32[]{:S(2)}) %all-to-all-start.1) | async-done | bytes 33554464 | tf_op jit(solution)/shard_map/all_to_all | solution.py:16
  1181.0 22.9 %copy.25 = bf16[16,2,16,64,512]{4,3,2,1,0:T(8,128)(2,1)} copy(bf16[16,2,16,64,512]{4,3,1,0,2:T(8,128)(2,1)} %bitcast.11) | data formatting | bytes 67108864 | tf_op jit(solution)/shard_map/reshape | solution.py:17
  1203.9 18.7 %bitcast_multiply_fusion = f32[64,2,16,1024]{3,0,1,2:T(8,128)} fusion(f32[64,1024]{1,0:T(8,128)S(1)} %compare_select_fusion, bf16[16,2,1024,512,1]{3,2,1,4,0:T(8,128)(2,1)} %bitcast.45, bf16[1,16,2,64,512]{4,3,2,0,1:T(8,128)(2,1)} %maximum_bitcast_fusion, bf16[1,16,2,64,512]{4,3,2,0,1:T(8,128)(2,1)S(1)} %bitcast.48), kind=kOutput, calls=%fused_computation.6 | convolution fusion | flops 4305453056 | bytes 46399488 | tf_op jit(solution)/shard_map/osrit,srjt->iosj/dot_general | solution.py:57
  1222.7 11.6 copy.26
  (18 shorter events, 2.7 us)
Async XLA Ops:
  1.8 493.5 %copy-start.1 = (f32[128]{0:T(128)S(1)}, f32[128]{0:T(128)}, u32[]{:S(2)}) copy-start(f32[128]{0:T(128)} %compare_select_fusion.1) | copy-start | bytes 1540
  1.8 493.5 %copy-start.2 = (s32[128]{0:T(128)S(1)}, s32[128]{0:T(128)}, u32[]{:S(2)}) copy-start(s32[128]{0:T(128)} %fusion.20) | copy-start | bytes 1540
  555.5 8.0 copy-start
  555.5 625.6 %all-to-all-start.1 = ((bf16[16,16,2,64,512]{4,3,2,1,0:T(8,128)(2,1)}), bf16[16,16,2,64,512]{4,3,2,1,0:T(8,128)(2,1)}, u32[]{:S(2)}, u32[]{:S(2)}) async-start(bf16[16,16,2,64,512]{4,3,2,1,0:T(8,128)(2,1)} %stack.64), calls=%async_computation.1 | async-start | bytes 67108864 | tf_op jit(solution)/shard_map/all_to_all | solution.py:16
